TPU v7x, 512 devices: a whole 4x4x16 slice. The times are simulated.
512 devices in a mesh: section: 16 (over y, x_hi, core), seq: 32 (over x_lo, z).
Axes of the slice: x: 4 (x_hi: 2, x_lo: 2; x = x_hi * 2 + x_lo), y: 4, z: 16, core: 2. Of those that a mesh axis runs over, the one named last changes fastest.
Arguments:
- saved_input: bfloat16 [16, 4096, 4096], P('section', 'seq'), may hold values from -6 to 6
- norm_gain: float32 [16, 4096], P('section'), may hold values from 0.25 to 1.75
- down_proj: bfloat16 [16, 4096, 512], P('section', 'seq'), may hold values from -0.09375 to 0.09375
- up_proj: bfloat16 [16, 512, 4096], P('section', None, 'seq'), may hold values from -0.25 to 0.25
- left_in: bfloat16 [16, 4096, 128], P('section', 'seq'), may hold values from -0.5 to 0.5
- right_in: bfloat16 [16, 4096, 128], P('section', 'seq'), may hold values from -6 to 6
- warm_right: bfloat16 [16, 4096, 128], P('section', 'seq'), may hold values from -6 to 6
- error_buffer: bfloat16 [16, 4096, 4096], P('section', 'seq'), may hold values from -4 to 4
- pair_lengths: int32 [16, 2], P('section'), may hold values from 512 to 2048, as said below
Outputs:
- new_error: bfloat16 [16, 4096, 4096], P('section', 'seq')
- left_out: bfloat16 [16, 4096, 128], P('section', 'seq')
- right_out: bfloat16 [16, 4096, 128], P('section', 'seq')
Inputs may be any that keep to these rules, and one draw needn't show every extreme that they name: `pair_lengths`: in each section one of the two sequences has the full length 2048.
All inputs are finite; a program needn't handle non-finite values.
Results may differ from a plain program's by a relative error of at most 0.025.
Values may be sent and summed in bfloat16 or wider, within the bound.
A program may use at most 64 MiB of HBM per device.

v0:
```python
import jax
import jax.numpy as jnp
from jax import lax
from jax.sharding import PartitionSpec as P


def from_behind(x, axis, by):
    size = lax.axis_size(axis)
    pairs = [(i, i + by) for i in range(size) if 0 <= i + by < size]
    return lax.ppermute(x, axis, pairs)


def contract_last(left, right):
    return lax.dot_general(
        left, right, (((1,), (1,)), ((), ())), preferred_element_type=jnp.float32
    )


def contract_first(left, right):
    return lax.dot_general(
        left, right, (((0,), (0,)), ((), ())), preferred_element_type=jnp.float32
    )


def per_device(
    saved_input,
    norm_gain,
    down_proj,
    up_proj,
    left_in,
    right_in,
    warm_right,
    error_buffer,
    pair_lengths,
):
    saved = saved_input[0]
    gain = norm_gain[0]
    lengths = pair_lengths[0]
    group_size = lax.axis_size("seq")
    group_index = lax.axis_index("seq")
    right_full_in, warm_full = (
        lax.all_gather(right_in[0], "seq", axis=0, tiled=True),
        lax.all_gather(warm_right[0], "seq", axis=0, tiled=True),
    )
    down_full, upper_full = (
        lax.all_gather(down_proj[0], "seq", axis=0, tiled=True),
        lax.all_gather(up_proj[0], "seq", axis=1, tiled=True),
    )
    wide_input = saved.astype(jnp.float32)
    inv_rms = lax.rsqrt(jnp.mean(wide_input * wide_input, axis=-1, keepdims=True) + 1e-05)
    unit_rows = wide_input * inv_rms
    normed = (unit_rows * gain).astype(jnp.bfloat16)
    ghat = contract_last(left_in[0], right_full_in)
    branch_pre = jnp.dot(normed, down_full, preferred_element_type=jnp.float32)
    dact = contract_last(ghat.astype(jnp.bfloat16), upper_full)
    gate_sig = jax.nn.sigmoid(branch_pre)
    dpre = (dact * gate_sig * (1.0 + branch_pre * (1.0 - gate_sig))).astype(jnp.bfloat16)
    dnormed = contract_last(dpre, down_full)
    dunit = dnormed * gain
    dnorm = inv_rms * (dunit - unit_rows * jnp.mean(dunit * unit_rows, axis=-1, keepdims=True))
    local_rows = saved.shape[0]
    seq_slots = local_rows * group_size // 2
    position = group_index * local_rows + jnp.arange(local_rows, dtype=jnp.int32)
    which_seq = position // seq_slots
    within = position % seq_slots
    limit = jnp.where(which_seq == 0, lengths[0], lengths[1])
    live_rows = (within < limit).astype(jnp.float32)[:, None]
    moment = live_rows * (ghat + dnorm + error_buffer[0].astype(jnp.float32))
    moment16 = moment.astype(jnp.bfloat16)
    projected = jnp.dot(moment16, warm_full, preferred_element_type=jnp.float32)
    local_gram = jnp.dot(projected.T, projected, precision=lax.Precision.HIGHEST)
    gram_matrix = lax.psum(local_gram, "seq")
    lower_factor = jnp.linalg.cholesky(gram_matrix)
    phat = lax.linalg.triangular_solve(
        lower_factor, projected, left_side=False, lower=True, transpose_a=True
    )
    phat16 = phat.astype(jnp.bfloat16)
    shard_sum = lax.psum_scatter(
        contract_first(moment16, phat16).astype(jnp.bfloat16),
        "seq",
        scatter_dimension=0,
        tiled=True,
    )
    right16 = lax.all_gather(shard_sum, "seq", axis=0, tiled=True)
    approx = contract_last(phat16, right16)
    new_error = (moment - approx).astype(jnp.bfloat16)
    left_back, right_back = from_behind((phat16, shard_sum), "section", -1)
    return (new_error[None], left_back[None], right_back[None])


def solution(mesh):
    return jax.shard_map(
        per_device,
        mesh=mesh,
        in_specs=(
            P("section", "seq", None),
            P("section", None),
            P("section", "seq", None),
            P("section", None, "seq"),
            P("section", "seq", None),
            P("section", "seq", None),
            P("section", "seq", None),
            P("section", "seq", None),
            P("section", None),
        ),
        out_specs=(P("section", "seq", None), P("section", "seq", None), P("section", "seq", None)),
        check_vma=False,
    )
```

profile of v0, /device:TPU:6, one launch (start us, length us, event | category | flops | bytes accessed | tf_op | source)
XLA Modules:
  0.0 1075.4 jit_solution(512663745190658282)
XLA Ops:
  7.2 0.0 copy-start
  7.2 0.0 all-gather.12.cloned.1.call-start
  7.2 0.7 all-gather.12.cloned.1.call-update
  7.9 0.0 all-gather.16.cloned.1.call-start
  8.0 0.7 all-gather.16.cloned.1.call-update
  8.7 0.0 all-gather.14.cloned.1.call-start
  8.7 0.7 all-gather.14.cloned.1.call-update
  9.4 0.0 all-gather.18.cloned.1.call-start
  9.4 0.5 all-gather.18.cloned.1.call-update
  10.0 0.0 all-reduce.2.cloned.1.call-start
  10.0 0.0 copy-start.2
  10.0 0.0 copy-start.3
  10.0 1.6 fusion.17
  11.7 1.3 fusion.55
  13.0 1.3 compare_convert_fusion
  14.3 131.4 %all-gather.12.cloned.1.call-done = bf16[1,4096,128]{2,1,0:T(8,128)(2,1)} async-done(((bf16[1,128,128]{2,1,0:T(8,128)(2,1)}), bf16[1,4096,128]{2,1,0:T(8,128)(2,1)}) %all-gather.12.cloned.1.call-update) | async-done | bytes 1048592 | tf_op jit(solution)/shard_map/all_gather | solution.py:42
  145.7 0.0 copy-done
  145.7 1.7 fusion.31
  147.4 0.0 copy-start.1
  147.4 131.6 %all-gather.16.cloned.1.call-done = bf16[1,4096,512]{2,1,0:T(8,128)(2,1)} async-done(((bf16[1,128,512]{2,1,0:T(8,128)(2,1)}), bf16[1,4096,512]{2,1,0:T(8,128)(2,1)}) %all-gather.16.cloned.1.call-update) | async-done | bytes 4194320 | tf_op jit(solution)/shard_map/all_gather | solution.py:46
  279.0 0.0 copy-done.2
  279.0 0.0 copy-done.3
  279.0 2.9 fusion.3
  281.9 134.9 %all-gather.14.cloned.1.call-done = bf16[1,512,4096]{2,1,0:T(8,128)(2,1)} async-done(((bf16[1,512,128]{2,1,0:T(8,128)(2,1)}), bf16[1,512,4096]{2,1,0:T(8,128)(2,1)}) %all-gather.14.cloned.1.call-update) | async-done | bytes 4194320 | tf_op jit(solution)/shard_map/all_gather | solution.py:47
  416.8 0.0 copy-done.1
  416.8 7.7 fusion.11
  424.5 3.3 fusion.16
  427.8 117.9 %all-gather.18.cloned.1.call-done = bf16[1,4096,128]{2,1,0:T(8,128)(2,1)} async-done(((bf16[1,128,128]{2,1,0:T(8,128)(2,1)}), bf16[1,4096,128]{2,1,0:T(8,128)(2,1)}) %all-gather.18.cloned.1.call-update) | async-done | bytes 1048592 | tf_op jit(solution)/shard_map/all_gather | solution.py:43
  545.7 1.6 fusion.28
  547.3 0.9 fusion.60
  548.2 0.0 all-reduce.2.cloned.1.call-update
  548.3 0.0 reduce-scatter.2.cloned.1.call-start
  548.3 225.9 %all-reduce.2.cloned.1.call-done = f32[128,128]{0,1:T(8,128)} async-done(((f32[128,128]{0,1:T(8,128)}), f32[128,128]{0,1:T(8,128)}) %all-reduce.2.cloned.1.call-update) | async-done | bytes 65552 | tf_op jit(solution)/shard_map/psum | solution.py:72
  774.2 0.9 copy.13
  775.2 0.9 fusion.52
  776.0 11.7 %cholesky.16 = f32[128,128]{1,0:T(8,128)S(1)} custom-call(f32[128,128]{1,0:T(8,128)S(1)} %fusion.52), custom_call_target="Cholesky" | custom-call | tf_op jit(solution)/shard_map/jit(cholesky)/cholesky | solution.py:73
  787.8 0.6 compare_reduce_fusion
  788.4 0.7 fusion.50
  789.1 9.8 custom-call.6
  798.9 0.2 convolution_convert_fusion.1
  799.1 1.4 convolution_convert_fusion
  800.6 0.0 reduce-scatter.2.cloned.1.call-update
  800.6 0.0 all-gather.10.cloned.1.call-start
  800.6 139.2 %reduce-scatter.2.cloned.1.call-done = bf16[128,128]{1,0:T(8,128)(2,1)} async-done(((bf16[4096,128]{1,0:T(8,128)(2,1)}), bf16[128,128]{1,0:T(8,128)(2,1)}) %reduce-scatter.2.cloned.1.call-update) | async-done | bytes 32784 | tf_op jit(solution)/shard_map/reduce_scatter | solution.py:78
  939.9 0.0 all-gather.10.cloned.1.call-update
  939.9 1.9 collective-permute-start
  941.8 3.2 collective-permute-start.1
  945.0 0.0 collective-permute-done
  945.0 1.9 collective-permute-done.1
  946.9 117.9 %all-gather.10.cloned.1.call-done = bf16[4096,128]{1,0:T(8,128)(2,1)} async-done(((bf16[128,128]{1,0:T(8,128)(2,1)}), bf16[4096,128]{1,0:T(8,128)(2,1)}) %all-gather.10.cloned.1.call-update) | async-done | bytes 1048592 | tf_op jit(solution)/shard_map/all_gather | solution.py:84
  1064.7 2.6 fusion.1
  1067.4 0.6 copy.18
  1068.0 0.6 copy.19
  (3 shorter events, 0.1 us)
Async XLA Ops:
  7.2 138.6 %copy-start = (bf16[1,128,128]{2,1,0:T(8,128)(2,1)S(1)}, bf16[1,128,128]{2,1,0:T(8,128)(2,1)}, u32[]{:S(2)}) copy-start(bf16[1,128,128]{2,1,0:T(8,128)(2,1)} %param.13) | copy-start | bytes 98308
  7.2 138.5 %all-gather.12.cloned.1.call-start = ((), (), s32[]{:S(2)}) async-start(), calls=%async_computation.4 | async-start | bytes 1081344 | tf_op jit(solution)/shard_map/all_gather | solution.py:42
  7.9 271.1 %all-gather.16.cloned.1.call-start = ((), (), s32[]{:S(2)}) async-start(), calls=%async_computation.6 | async-start | bytes 4325376 | tf_op jit(solution)/shard_map/all_gather | solution.py:46
  8.7 408.1 %all-gather.14.cloned.1.call-start = ((), (), s32[]{:S(2)}) async-start(), calls=%async_computation.5 | async-start | bytes 4325376 | tf_op jit(solution)/shard_map/all_gather | solution.py:47
  9.4 536.3 %all-gather.18.cloned.1.call-start = ((), (), s32[]{:S(2)}) async-start(), calls=%async_computation.7 | async-start | bytes 1081344 | tf_op jit(solution)/shard_map/all_gather | solution.py:43
  10.0 764.3 %all-reduce.2.cloned.1.call-start = ((), (), s32[]{:S(2)}) async-start(), calls=%async_computation.1 | async-start | bytes 131072 | tf_op jit(solution)/shard_map/psum | solution.py:72
  10.0 269.0 %copy-start.2 = (bf16[1,128,4096]{2,1,0:T(8,128)(2,1)S(1)}, bf16[1,128,4096]{2,1,0:T(8,128)(2,1)}, u32[]{:S(2)}) copy-start(bf16[1,128,4096]{2,1,0:T(8,128)(2,1)} %param.9) | copy-start | bytes 3145732
  10.0 269.0 %copy-start.3 = (f32[1,4096]{1,0:T(1,128)S(1)}, f32[1,4096]{1,0:T(1,128)}, u32[]{:S(2)}) copy-start(f32[1,4096]{1,0:T(1,128)} %param.10) | copy-start | bytes 49156
  147.4 269.4 %copy-start.1 = (f32[128,4096]{1,0:T(8,128)}, f32[128,4096]{1,0:T(8,128)S(1)}, u32[]{:S(2)}) copy-start(f32[128,4096]{1,0:T(8,128)S(1)} %fusion.31) | copy-start | bytes 6291460
  548.3 391.6 %reduce-scatter.2.cloned.1.call-start = ((), (), s32[]{:S(2)}) async-start(), calls=%async_computation.2 | async-start | bytes 1081344 | tf_op jit(solution)/shard_map/reduce_scatter | solution.py:78
  800.6 264.2 %all-gather.10.cloned.1.call-start = ((), (), s32[]{:S(2)}) async-start(), calls=%async_computation.3 | async-start | bytes 1081344 | tf_op jit(solution)/shard_map/all_gather | solution.py:84
  939.9 5.1 collective-permute-start
  941.8 5.1 collective-permute-start.1
Sparse Core Ops, SparseCore 0:
  10.1 135.5 all-gather.11
  147.8 131.1 all-gather.15
  281.0 135.7 all-gather.13
  418.7 126.8 all-gather.17
  549.0 225.1 all-reduce.1
  800.7 139.1 reduce-scatter.1
  941.9 122.7 all-gather.9
where the time goes:
time: 1080 us
  waiting for transfers between devices  1000 us (93%)
  other arithmetic  29.9 us (3%)
  matrix products  19.2 us (2%)
  between operations  14.3 us (1%)
    psum x1, waiting for transfers between devices, per_device(): gram_matrix = lax.psum(local_gram, 'seq')  226 us
    reduce_scatter x1, waiting for transfers between devices, per_device(): lax.psum_scatter(contract_first(moment16, phat16).astype(jnp.bfloat16), '...  139 us
    all_gather x1, waiting for transfers between devices, per_device(): lax.all_gather(up_proj[0], 'seq', axis=1, tiled=True)  135 us
    all_gather x1, waiting for transfers between devices, per_device(): lax.all_gather(down_proj[0], 'seq', axis=0, tiled=True)  132 us
    all_gather x1, waiting for transfers between devices, per_device(): lax.all_gather(right_in[0], 'seq', axis=0, tiled=True)  131 us
    all_gather x1, waiting for transfers between devices, per_device(): right16 = lax.all_gather(shard_sum, 'seq', axis=0, tiled=True)  118 us
    all_gather x1, waiting for transfers between devices, per_device(): lax.all_gather(warm_right[0], 'seq', axis=0, tiled=True)  118 us
  transfers between devices with their start and end apart: 9, of which 8 were waited for; matrix products, arithmetic and copies ran while one was open for 2% of the time, Pallas kernels for 0%

commit v1 on v0

v1 whole, which is shorter than its diff:
```python
import functools

import jax
import jax.numpy as jnp
from jax import lax
from jax.experimental import pallas as pl
from jax.experimental.pallas import tpu as pltpu
from jax.sharding import PartitionSpec as P

MESH = pl.DeviceIdType.MESH
HIGHEST = lax.Precision.HIGHEST
F32 = jnp.float32
BF16 = jnp.bfloat16
RIGHT, LEFT = 0, 1


def nt(a, b, precision=None):
    return lax.dot_general(
        a, b, (((1,), (1,)), ((), ())), preferred_element_type=F32, precision=precision
    )


def nn(a, b, precision=None):
    return jnp.dot(a, b, preferred_element_type=F32, precision=precision)


def split(a):
    hi = a.astype(BF16)
    return hi, (a - hi.astype(F32)).astype(BF16)


def kernel(
    n_section, nz, rank, lens, gain_in, saved, err, down, up, left, right, warm,
    out_ne, out_l, out_r,
    gain, xall, xoth, eall, lall, upv, dall, rw, ivb,
    mpart, ml1, m2s, ml2, mxs, mxr, mown, mfull,
    xg, prs, prr, pre_ref, dpre_ref, mom, mom16, pjs, pjr, pj,
    gpart, gl1, g2s, gl2, gfull, work, linv, ut, ula, ulb, u2s, un, ul2, rt, ph16, rown, neb,
    ld_sem, x_send, x_recv, a_send, a_recv,
    m_send, m_recv, g_send, g_recv, u_send, u_recv, r_send, r_recv, q_send, q_recv,
    ne_send, ne_recv, ne_loc, sec_send, sec_recv,
):
    tok = left.shape[0]
    feat = saved.shape[1]
    half = feat // 2
    steps = nz // 2
    chunk = 2 * tok
    n_chunk = half // chunk
    rl = down.shape[1]
    nb = 4
    na = nz // nb

    s = lax.axis_index("section")
    q = lax.axis_index("seq")
    x = q // nz
    z = lax.rem(q, nz)
    a = z // nb
    b = lax.rem(z, nb)
    o = 1 - x
    base = x * nz
    partner = o * nz + z
    zr = base + lax.rem(z + 1, nz)
    zl = base + lax.rem(z + nz - 1, nz)
    s_prev = lax.rem(s + n_section - 1, n_section)
    s_next = lax.rem(s + 1, n_section)

    def mod(i):
        return lax.rem(i + 2 * nz, nz)

    def rows(start, size):
        return pl.ds(pl.multiple_of(start, size), size)

    def near_b(k):
        return lax.rem(b + k, nb)

    def far_a(k):
        return lax.rem(a + k, na)

    mine = rows(x * tok, tok)
    theirs = rows(o * tok, tok)
    my_half = rows(x * half, half)
    other_half = rows(o * half, half)
    my_block = rows(z * tok, tok)

    loads = [
        pltpu.make_async_copy(src, dst, ld_sem.at[i])
        for i, (src, dst) in enumerate([
            (down, dall.at[my_block]),
            (right, rw.at[z, 0]),
            (warm, rw.at[z, 1]),
            (left, lall.at[mine]),
            (saved.at[:, other_half], xoth),
            (up, upv),
            (saved.at[:, my_half], xall.at[mine]),
            (err.at[:, my_half], eall.at[mine]),
            (gain_in, gain),
        ])
    ]
    for load in loads:
        load.start()

    barrier = pltpu.get_barrier_semaphore()
    peers = [{"seq": base + a * nb + near_b(k)} for k in range(1, nb)]
    peers += [{"seq": base + far_a(k) * nb + b} for k in range(1, na)]
    peers += [{"seq": zr}, {"seq": zl}, {"seq": partner}, {"section": s_prev}, {"section": s_next}]
    for peer in peers:
        pl.semaphore_signal(barrier, inc=1, device_id=peer, device_id_type=MESH)
    pl.semaphore_wait(barrier, len(peers))

    def send_to(device, src, dst, send, recv):
        return pltpu.make_async_remote_copy(
            src_ref=src, dst_ref=dst, send_sem=send, recv_sem=recv,
            device_id=device, device_id_type=MESH,
        )

    def across(i, src, dst):
        return send_to({"seq": partner}, src, dst, x_send.at[i], x_recv.at[i])

    def near(k, src, dst, send, recv):
        return send_to({"seq": base + a * nb + near_b(k)}, src, dst, send, recv)

    def far(k, src, dst, send, recv):
        return send_to({"seq": base + far_a(k) * nb + b}, src, dst, send, recv)

    def loop(first, end, fn):
        def body(k, _):
            fn(k)
            return 0

        lax.fori_loop(first, end, body, 0)

    longer = [(0, RIGHT), (1, LEFT)]

    def hop(stream, way, step):
        block = mod(z - step) if way == RIGHT else mod(z + step)
        ref = dall.at[rows(block * tok, tok)] if stream == 0 else rw.at[block]
        return send_to(
            {"seq": zr if way == RIGHT else zl}, ref, ref,
            a_send.at[stream, way, step], a_recv.at[stream, way, step],
        )

    def has(stream, way, step):
        return step < (steps if (stream, way) in longer else steps - 1)

    def advance(stream, step):
        for way in (RIGHT, LEFT):
            if has(stream, way, step):
                hop(stream, way, step).wait_recv()
                if has(stream, way, step + 1):
                    hop(stream, way, step + 1).start()

    def ring_start(stream):
        for way in (RIGHT, LEFT):
            hop(stream, way, 0).start()

    loads[0].wait()
    ring_start(0)
    loads[1].wait()
    loads[2].wait()
    loads[3].wait()
    x_left = across(1, lall.at[mine], lall.at[mine])
    x_left.start()
    loads[4].wait()
    x_saved = across(0, xoth, xall.at[mine])
    x_saved.start()
    loads[5].wait()

    mb, ms = rl // nb, rl // nz
    mpart[...] = nn(upv[...], rw[z, 0]).astype(BF16)
    my_m = rows(b * mb + a * ms, ms)
    my_mb = rows(b * mb, mb)
    m1 = [near(k, mpart.at[rows(near_b(k) * mb, mb)], ml1.at[k], m_send.at[0, k], m_recv.at[0, k])
          for k in range(1, nb)]
    m2 = [far(k, m2s.at[rows(far_a(k) * ms, ms)], ml2.at[k], m_send.at[1, k], m_recv.at[1, k])
          for k in range(1, na)]
    m3 = [far(k, mown, mfull.at[my_m], m_send.at[2, k], m_recv.at[2, k]) for k in range(1, na)]
    m4 = [near(k, mfull.at[my_mb], mfull.at[my_mb], m_send.at[3, k], m_recv.at[3, k])
          for k in range(1, nb)]

    def start(copies):
        for copy in copies:
            copy.start()

    def arrive(copies):
        for copy in copies:
            copy.wait_recv()

    start(m1)
    x_err = across(2, err.at[:, other_half], eall.at[mine])
    x_err.start()

    loads[6].wait()
    total = jnp.zeros((tok, 1), F32)
    for c in range(half // 512):
        cols = pl.ds(c * 512, 512)
        for v in (xoth[:, cols], xall[mine, cols]):
            v = v.astype(F32)
            total = total + jnp.sum(v * v, axis=1, keepdims=True)
    ivb[mine, :] = jnp.broadcast_to(lax.rsqrt(total * (1.0 / feat) + 1e-05), (tok, 128))
    x_inv = across(3, ivb.at[mine], ivb.at[mine])
    x_inv.start()

    gain_off = x * half

    def scale(c):
        cols = rows(c * chunk, chunk)
        g = gain[:, rows(gain_off + c * chunk, chunk)]
        xg[:, cols] = (xall[:, cols].astype(F32) * g).astype(BF16)

    def term(block):
        return nn(xg[:, rows(block * tok, tok)], dall[rows(block * tok, tok), :])

    def blocks_of(step):
        if step < 0:
            return [z]
        if step == steps - 1:
            return [mod(z - steps)]
        return [mod(z - 1 - step), mod(z + 1 + step)]

    lag = 3 * steps // 8
    for t in range(steps):
        if t == lag:
            ring_start(1)
        advance(0, t)
        if t >= lag:
            advance(1, t - lag)
        if t == steps // 8:
            arrive(m1)
            msum = mpart[my_mb, :].astype(F32)
            for k in range(1, nb):
                msum = msum + ml1[k].astype(F32)
            m2s[...] = msum.astype(BF16)
            start(m2)
        if t == 3 * steps // 8:
            arrive(m2)
            msum = m2s[rows(a * ms, ms), :].astype(F32)
            for k in range(1, na):
                msum = msum + ml2[k].astype(F32)
            mxs[...] = msum
            x_m = across(4, mxs, mxr)
            x_m.start()
        if t == steps // 2:
            x_saved.wait_recv()
            loads[8].wait()
            loop(0, n_chunk, scale)
            pre_ref[...] = term(z)
        if t == 5 * steps // 8:
            x_m.wait_recv()
            mown[...] = (mxs[...] + mxr[...]).astype(BF16)
            mfull[my_m, :] = mown[...]
            start(m3)
        if t == 6 * steps // 8:
            arrive(m3)
            start(m4)
        if t >= steps // 2:
            first = 2 * (t - steps // 2)
            found = [term(block) for step in (first, first + 1) for block in blocks_of(step)]
            pre_own = pre_ref[...] + sum(found[1:], found[0])
            pre_ref[...] = pre_own
    prs[...] = pre_own.astype(BF16)
    x_pre = across(5, prs, prr)
    x_pre.start()

    x_left.wait_recv()
    share = -(-(steps + 1) // lag)
    for i in range(lag):
        advance(1, steps - lag + i)
        for step in range(i * share - 1, min((i + 1) * share, steps + 1) - 1):
            for block in blocks_of(step):
                mom[:, rows(block * tok, tok)] = nt(lall[...], rw[block, 0])
    x_inv.wait_recv()
    arrive(m4)
    dact = nt(lall[...], mfull[...])
    inv = ivb[:, 0:1]
    slot = z * tok + lax.broadcasted_iota(jnp.int32, (2 * tok, 1), 0)
    second = lax.broadcasted_iota(jnp.int32, (2 * tok, 1), 0) >= tok
    limit = jnp.where(second, lens[0, 1] + tok, lens[0, 0])
    live = jnp.where(slot < limit, 1.0, 0.0).astype(F32)

    loads[7].wait()
    x_err.wait_recv()
    x_pre.wait_recv()
    pre = inv * (pre_ref[...] + prr[...].astype(F32))
    sg = 1.0 / (1.0 + jnp.exp(-pre))
    dpre = (dact * sg * (1.0 + pre * (1.0 - sg))).astype(BF16)
    dpre_ref[...] = dpre
    mean = jnp.sum(dpre.astype(F32) * pre, axis=1, keepdims=True) * (1.0 / feat)
    back = inv * inv * mean
    pjs[...] = jnp.zeros_like(pjs)

    def momentum(c):
        cols = rows(c * chunk, chunk)
        g = gain[:, rows(gain_off + c * chunk, chunk)]
        dn = nt(dpre_ref[...], dall[cols, :])
        m = mom[:, cols] + eall[:, cols].astype(F32)
        m = live * (m + inv * (dn * g) - xall[:, cols].astype(F32) * back)
        mom[:, cols] = m
        m16 = m.astype(BF16)
        mom16[:, cols] = m16
        pjs[...] += nn(m16, rw[pl.ds(2 * c, 2), 1].reshape(chunk, rank))

    loop(0, n_chunk, momentum)
    x_pj = across(6, pjs, pjr)
    x_pj.start()
    x_pj.wait_recv()
    proj = pjs[...] + pjr[...]
    pj[...] = proj
    proj_t = proj.T

    gb = rank // nb
    my_gb = rows(b * gb, gb)
    gpart[...] = nn(proj_t, proj, HIGHEST)
    g1 = [near(k, gpart.at[rows(near_b(k) * gb, gb)], gl1.at[k], g_send.at[0, k], g_recv.at[0, k])
          for k in range(1, nb)]
    g2 = [far(k, g2s, gl2.at[k], g_send.at[1, k], g_recv.at[1, k]) for k in range(1, na)]
    g3 = [near(k, gfull.at[my_gb], gfull.at[my_gb], g_send.at[2, k], g_recv.at[2, k])
          for k in range(1, nb)]
    start(g1)

    hi, lo = split(proj_t)

    def moment_terms(j):
        residue = near_b(j)

        def terms(i):
            m = mom16[:, rows((i * nb + residue) * tok, tok)]
            ut[residue, i] = nn(hi, m) + nn(lo, m)

        loop(0, na, terms)

    first_half, last_half = pl.ds(0, na // 2), pl.ds(na // 2, na // 2)
    to_right, to_left = {"seq": zr}, {"seq": zl}
    ua = [
        send_to(to_right, ut.at[near_b(2), first_half], ula.at[0], u_send.at[0], u_recv.at[0]),
        send_to(to_left, ut.at[near_b(2), last_half], ula.at[1], u_send.at[1], u_recv.at[1]),
    ]
    ub = [
        send_to(to_right, ut.at[near_b(1)], ulb.at[0], u_send.at[2], u_recv.at[2]),
        send_to(to_left, ut.at[near_b(3)], ulb.at[1], u_send.at[3], u_recv.at[3]),
    ]
    u2 = [far(k, un.at[far_a(k)], ul2.at[k], u_send.at[3 + k], u_recv.at[3 + k])
          for k in range(1, na)]

    moment_terms(2)
    start(ua)
    arrive(g1)
    gsum = gpart[my_gb, :]
    for k in range(1, nb):
        gsum = gsum + gl1[k]
    g2s[...] = gsum
    start(g2)
    moment_terms(1)
    moment_terms(3)
    arrive(g2)
    gsum = g2s[...]
    for k in range(1, na):
        gsum = gsum + gl2[k]
    gfull[my_gb, :] = gsum
    start(g3)
    arrive(ua)
    ut[near_b(1), first_half] += ula[0]
    ut[near_b(3), last_half] += ula[1]
    start(ub)
    moment_terms(0)
    arrive(g3)
    work[...] = gfull[...]

    lane = lax.broadcasted_iota(jnp.int32, (1, rank), 1)
    group, width = 16, 8

    def eliminate(first, width):
        n = rank - first
        a = work[pl.ds(first, n), :]
        index = lax.broadcasted_iota(jnp.int32, (n, rank), 0)
        cols = [
            jnp.broadcast_to(a[:, first + k : first + k + 1], (n, rank)) for k in range(width)
        ]
        panel = a[0:8, :]
        rest = jnp.where((lane >= first) & (lane < first + width), 0.0, a)
        for k in range(width):
            here = lane == first + k
            pivot = cols[k][k : k + 1, :]
            factor = jnp.where(index > k, cols[k] * (1.0 / pivot), 0.0)
            unit = jnp.where(here, 1.0, panel[k : k + 1, :])
            linv[first + k : first + k + 1, :] = (
                jnp.where(lane <= first + k, unit, 0.0) * lax.rsqrt(pivot)
            )
            if k + 1 < width:
                panel = jnp.where(here, 0.0, panel) - factor[0:8, :] * unit
            for later in range(k + 1, width):
                cols[later] = cols[later] - factor * cols[k][later : later + 1, :]
            inside = (lane > first + k) & (lane < first + width)
            rest = rest - factor * jnp.where(inside, 0.0, unit)
        if n > width:
            work[pl.ds(first + width, n - width), :] = rest[width:, :]

    for first in range(0, rank // 2, width):
        eliminate(first, width)

    arrive(ub)
    u2s[...] = ut[b] + ulb[0] + ulb[1]
    for first in range(rank // 2, rank, width):
        eliminate(first, width)

    li = linv[...]
    for k in (*range(na // 2, na), *range(1, na // 2), 0):
        un[far_a(k)] = nn(li, u2s[far_a(k)], HIGHEST).astype(BF16)
        if k > 0:
            u2[k - 1].start()
    ph16[...] = nt(pj[...], li, HIGHEST).astype(BF16)
    to_prev = {"section": s_prev}
    outs = [
        send_to(to_prev, ph16.at[mine], out_l, sec_send.at[0], sec_recv.at[0]),
        send_to(to_prev, rown, out_r, sec_send.at[1], sec_recv.at[1]),
    ]
    outs[0].start()
    arrive(u2)
    right_t = un[a].astype(F32)
    for k in range(1, na):
        right_t = right_t + ul2[k].astype(F32)
    rt[b, a] = right_t.astype(BF16)

    r1 = [far(k, rt.at[b, a], rt.at[b, a], r_send.at[k], r_recv.at[k]) for k in range(1, na)]

    def pass_on(device, view, i):
        return send_to(device, rt.at[view], rt.at[view], q_send.at[i], q_recv.at[i])

    rb_right = [pass_on(to_right, (b, first_half), 0), pass_on(to_right, (b, last_half), 1)]
    rb_left = [pass_on(to_left, (b, first_half), 2), pass_on(to_left, (b, last_half), 3)]
    rc_right = pass_on(to_right, (near_b(3), first_half), 4)
    rc_left = pass_on(to_left, (near_b(1), last_half), 5)
    start(r1)
    rown[...] = right_t.T.astype(BF16)
    outs[1].start()
    arrive(r1)
    start([rb_right[0], rb_left[1], rb_right[1], rb_left[0]])

    def finished(block):
        cols = rows(block * tok, tok)
        return send_to(
            {"seq": partner}, neb.at[theirs, cols], out_ne.at[:, rows(x * half + block * tok, tok)],
            ne_send.at[block], ne_recv.at[block],
        )

    def finish(j, first, end):
        residue = near_b(j)

        def one(i):
            block = i * nb + residue
            cols = rows(block * tok, tok)
            approx = nn(ph16[...], rt[residue, i])
            neb[:, cols] = (mom[:, cols] - approx).astype(BF16)
            finished(block).start()

        loop(first, end, one)

    finish(0, 0, na)
    rb_right[0].wait_recv()
    rc_right.start()
    rb_left[1].wait_recv()
    rc_left.start()
    rb_right[1].wait_recv()
    finish(3, 0, na)
    rb_left[0].wait_recv()
    finish(1, 0, na)
    rc_right.wait_recv()
    finish(2, 0, na // 2)
    rc_left.wait_recv()
    finish(2, na // 2, na)
    own = pltpu.make_async_copy(neb.at[mine], out_ne.at[:, my_half], ne_loc)
    own.start()

    for copy in (x_saved, x_left, x_err, x_inv, x_m, x_pre, x_pj):
        copy.wait_send()
    for copies in (
        m1, m2, m3, m4, g1, g2, g3, ua, ub, u2, r1, rb_right, rb_left, [rc_right, rc_left],
    ):
        for copy in copies:
            copy.wait_send()

    def drain(step):
        for stream in (0, 1):
            for way in (RIGHT, LEFT):
                hop(stream, way, step).wait_send()

    loop(0, steps - 1, drain)
    for pair in longer:
        hop(*pair, steps - 1).wait_send()
    for copy in outs:
        copy.wait()
    loop(0, nz, lambda block: finished(block).wait_send())
    loop(0, nz, lambda block: finished(block).wait_recv())
    own.wait()


def per_device(
    n_section, nz, saved_input, norm_gain, down_proj, up_proj, left_in, right_in, warm_right,
    error_buffer, pair_lengths,
):
    tok, feat = saved_input.shape[1:]
    rank = left_in.shape[2]
    rl = down_proj.shape[2]
    half = feat // 2
    steps = nz // 2
    nb = 4
    na = nz // nb
    hbm = pl.BlockSpec(memory_space=pl.ANY)
    dma = pltpu.SemaphoreType.DMA
    vmem = pltpu.VMEM
    scratch = [
        vmem((1, feat), F32),
        vmem((2 * tok, half), BF16),
        vmem((tok, half), BF16),
        vmem((2 * tok, half), BF16),
        vmem((2 * tok, rank), BF16),
        vmem((rl, tok), BF16),
        vmem((half, rl), BF16),
        vmem((nz, 2, tok, rank), BF16),
        vmem((2 * tok, 128), F32),
        vmem((rl, rank), BF16),
        vmem((nb, rl // nb, rank), BF16),
        vmem((rl // nb, rank), BF16),
        vmem((na, rl // nz, rank), BF16),
        vmem((rl // nz, rank), F32),
        vmem((rl // nz, rank), F32),
        vmem((rl // nz, rank), BF16),
        vmem((rl, rank), BF16),
        vmem((2 * tok, half), BF16),
        vmem((2 * tok, rl), BF16),
        vmem((2 * tok, rl), BF16),
        vmem((2 * tok, rl), F32),
        vmem((2 * tok, rl), BF16),
        vmem((2 * tok, half), F32),
        vmem((2 * tok, half), BF16),
        vmem((2 * tok, rank), F32),
        vmem((2 * tok, rank), F32),
        vmem((2 * tok, rank), F32),
        vmem((rank, rank), F32),
        vmem((nb, rank // nb, rank), F32),
        vmem((rank // nb, rank), F32),
        vmem((na, rank // nb, rank), F32),
        vmem((rank, rank), F32),
        vmem((rank, rank), F32),
        vmem((rank, rank), F32),
        vmem((nb, na, rank, tok), F32),
        vmem((2, na // 2, rank, tok), F32),
        vmem((2, na, rank, tok), F32),
        vmem((na, rank, tok), F32),
        vmem((na, rank, tok), BF16),
        vmem((na, rank, tok), BF16),
        vmem((nb, na, rank, tok), BF16),
        vmem((2 * tok, rank), BF16),
        vmem((tok, rank), BF16),
        vmem((2 * tok, half), BF16),
        dma((9,)), dma((7,)), dma((7,)),
        dma((2, 2, steps)), dma((2, 2, steps)),
        dma((4, 4)), dma((4, 4)), dma((4, 4)), dma((4, 4)),
        dma((8,)), dma((8,)), dma((4,)), dma((4,)), dma((6,)), dma((6,)),
        dma((nz,)), dma((nz,)), dma, dma((2,)), dma((2,)),
    ]
    new_error, left_back, right_back = pl.pallas_call(
        functools.partial(kernel, n_section, nz, rank),
        out_shape=(
            jax.ShapeDtypeStruct((tok, feat), BF16),
            jax.ShapeDtypeStruct((tok, rank), BF16),
            jax.ShapeDtypeStruct((tok, rank), BF16),
        ),
        in_specs=[
            pl.BlockSpec(memory_space=pltpu.SMEM), hbm,
            hbm, hbm, hbm, hbm, hbm, hbm, hbm,
        ],
        out_specs=(hbm, hbm, hbm),
        scratch_shapes=scratch,
        compiler_params=pltpu.CompilerParams(
            collective_id=0, has_side_effects=True, vmem_limit_bytes=60 * 1024 * 1024
        ),
    )(
        pair_lengths, norm_gain, saved_input[0], error_buffer[0], down_proj[0], up_proj[0],
        left_in[0], right_in[0], warm_right[0],
    )
    keep = lax.axis_index("section") < n_section - 1
    left_back = jnp.where(keep, left_back, jnp.zeros_like(left_back))
    right_back = jnp.where(keep, right_back, jnp.zeros_like(right_back))
    return (new_error[None], left_back[None], right_back[None])


def solution(mesh):
    n_section = mesh.shape["section"]
    nz = mesh.shape["seq"] // 2
    return jax.shard_map(
        functools.partial(per_device, n_section, nz),
        mesh=mesh,
        in_specs=(
            P("section", "seq", None),
            P("section", None),
            P("section", "seq", None),
            P("section", None, "seq"),
            P("section", "seq", None),
            P("section", "seq", None),
            P("section", "seq", None),
            P("section", "seq", None),
            P("section", None),
        ),
        out_specs=(P("section", "seq", None), P("section", "seq", None), P("section", "seq", None)),
        check_vma=False,
    )
```

time: 1080 us -> 136 us (0.13)
  waiting for transfers between devices: 1000 us -> 0 us
  Pallas kernels: 0 us -> 130 us
  other arithmetic: 29.9 us -> 1.41 us
  matrix products: 19.2 us -> 0 us
  between operations: 14.3 us -> 0.65 us
    all_gather x5 -> x0, waiting for transfers between devices: 634 us -> none  [the longest x1 135 us: per_device(): lax.all_gather(up_proj[0], 'seq', axis=1, tiled=True)]
    psum x1 -> x0, waiting for transfers between devices: 226 us -> none  [per_device(): gram_matrix = lax.psum(local_gram, 'seq')]
    reduce_scatter x1 -> x0, waiting for transfers between devices: 139 us -> none  [per_device(): lax.psum_scatter(contract_first(moment16, phat16).astype(jnp.bfloat16), '...]
    pallas_call x0 -> x1, Pallas kernels: none -> 130 us  [per_device(): pl.pallas_call(functools.partial(kernel, n_section, nz, rank), out_shape=...]
    another operation x5 -> x0, other arithmetic: 22.9 us -> none  [the longest x3 12.4 us: per_device(): lower_factor = jnp.linalg.cholesky(gram_matrix)]
    dot_general x7 -> x0, matrix products: 19 us -> none  [the longest x3 12 us: contract_last(): lax.dot_general(left, right, (((1,), (1,)), ((), ())), preferred_element_...]
  transfers between devices with their start and end apart: 9 -> 0, of which waited for: 8 -> 0; matrix products, arithmetic and copies ran while one was open for 2% -> 0% of each run, Pallas kernels for 0% -> 0%
where the time goes in v1:
time: 136 us; the launch traced here: 134 us
  Pallas kernels  130 us (96%)
  local copies, waits for them, and re-layouts  2.29 us (2%)
  other arithmetic  1.41 us (1%)
    pallas_call x1, Pallas kernels, per_device(): pl.pallas_call(functools.partial(kernel, n_section, nz, rank), out_shape=...  130 us

profile of v1, /device:TPU:6, one launch (start us, length us, event | category | flops | bytes accessed | tf_op | source)
XLA Modules:
  0.0 134.0 jit_solution(2681510831108886180)
XLA Ops:
  0.6 129.7 %shard_map.112 = (bf16[128,4096]{1,0:T(8,128)(2,1)}, bf16[128,128]{1,0:T(8,128)(2,1)}, bf16[128,128]{1,0:T(8,128)(2,1)}) custom-call(s32[1,2]{1,0:T(1,128)} %lens.1, f32[1,4096]{1,0:T(1,128)} %gain_in.1, bf16[128,4096]{1,0:T(8,128)(2,1)} %bitcast.12, bf16[128,4096]{1,0:T(8,128)(2,1)} %bitcast.13, bf16[128,512]{1,0:T(8,128)(2,1)} %bitcast.15, ...), custom_call_target="tpu_custom_call" | custom-call | tf_op jit(solution)/shard_map/pallas_call | solution.py:561
  130.3 1.4 %select_bitcast_fusion = (bf16[1,128,128]{2,1,0:T(8,128)(2,1)}, bf16[1,128,128]{2,1,0:T(8,128)(2,1)}) fusion(bf16[128,128]{1,0:T(8,128)(2,1)} %get-tuple-element.8, pred[]{:T(512)S(6)} %lt.3, bf16[128,128]{1,0:T(8,128)(2,1)} %get-tuple-element.7), kind=kLoop, calls=%fused_computation | loop fusion | flops 32768 | bytes 131073 | tf_op jit(solution)/shard_map/broadcast_in_dim | solution.py:584
  131.7 2.3 %copy.13 = bf16[1,128,4096]{2,1,0:T(8,128)(2,1)} copy(bf16[1,128,4096]{2,1,0:T(8,128)(2,1)} %bitcast.14) | data formatting | bytes 2097152

commit v2 on v1

--- a/solution.py
+++ b/solution.py
@@ -190,12 +190,16 @@
     x_err.start()
 
     loads[6].wait()
-    total = jnp.zeros((tok, 1), F32)
-    for c in range(half // 512):
-        cols = pl.ds(c * 512, 512)
+
+    def squares(c, total):
+        cols = rows(c * 128, 128)
         for v in (xoth[:, cols], xall[mine, cols]):
             v = v.astype(F32)
-            total = total + jnp.sum(v * v, axis=1, keepdims=True)
+            total = total + v * v
+        return total
+
+    total = lax.fori_loop(0, half // 128, squares, jnp.zeros((tok, 128), F32))
+    total = jnp.sum(total, axis=1, keepdims=True)
     ivb[mine, :] = jnp.broadcast_to(lax.rsqrt(total * (1.0 / feat) + 1e-05), (tok, 128))
     x_inv = across(3, ivb.at[mine], ivb.at[mine])
     x_inv.start()
@@ -210,12 +214,15 @@
     def term(block):
         return nn(xg[:, rows(block * tok, tok)], dall[rows(block * tok, tok), :])
 
-    def blocks_of(step):
-        if step < 0:
-            return [z]
-        if step == steps - 1:
-            return [mod(z - steps)]
-        return [mod(z - 1 - step), mod(z + 1 + step)]
+    def add_terms(step):
+        pre_ref[...] += term(mod(z - 1 - step)) + term(mod(z + 1 + step))
+
+    def gradient(block):
+        mom[:, rows(block * tok, tok)] = nt(lall[...], rw[block, 0])
+
+    def gradients(step):
+        gradient(mod(z - 1 - step))
+        gradient(mod(z + 1 + step))
 
     lag = 3 * steps // 8
     for t in range(steps):
@@ -254,20 +261,19 @@
             start(m4)
         if t >= steps // 2:
             first = 2 * (t - steps // 2)
-            found = [term(block) for step in (first, first + 1) for block in blocks_of(step)]
-            pre_own = pre_ref[...] + sum(found[1:], found[0])
-            pre_ref[...] = pre_own
+            loop(first, min(first + 2, steps - 1), add_terms)
+    pre_own = pre_ref[...] + term(mod(z - steps))
+    pre_ref[...] = pre_own
     prs[...] = pre_own.astype(BF16)
     x_pre = across(5, prs, prr)
     x_pre.start()
 
     x_left.wait_recv()
-    share = -(-(steps + 1) // lag)
+    gradient(z)
     for i in range(lag):
         advance(1, steps - lag + i)
-        for step in range(i * share - 1, min((i + 1) * share, steps + 1) - 1):
-            for block in blocks_of(step):
-                mom[:, rows(block * tok, tok)] = nt(lall[...], rw[block, 0])
+        loop(i * steps // lag, min((i + 1) * steps // lag, steps - 1), gradients)
+    gradient(mod(z - steps))
     x_inv.wait_recv()
     arrive(m4)
     dact = nt(lall[...], mfull[...])
@@ -366,41 +372,51 @@
     work[...] = gfull[...]
 
     lane = lax.broadcasted_iota(jnp.int32, (1, rank), 1)
-    group, width = 16, 8
-
-    def eliminate(first, width):
-        n = rank - first
-        a = work[pl.ds(first, n), :]
-        index = lax.broadcasted_iota(jnp.int32, (n, rank), 0)
-        cols = [
-            jnp.broadcast_to(a[:, first + k : first + k + 1], (n, rank)) for k in range(width)
+    width = 8
+
+    def eliminate(top, first):
+        n = rank - top
+        first = pl.multiple_of(first, width)
+        rest = work[top:, :]
+        panel = work[pl.ds(first, width), :]
+        index = top + lax.broadcasted_iota(jnp.int32, (n, rank), 0)
+        inner = lax.broadcasted_iota(jnp.int32, (width, rank), 0)
+        turned = pltpu.roll(rest, rank - first, 1)
+        turned_panel = pltpu.roll(panel, rank - first, 1)
+        cols = [jnp.broadcast_to(turned[:, k : k + 1], (n, rank)) for k in range(width)]
+        heads = [
+            jnp.broadcast_to(turned_panel[:, k : k + 1], (width, rank)) for k in range(width)
         ]
-        panel = a[0:8, :]
-        rest = jnp.where((lane >= first) & (lane < first + width), 0.0, a)
+        done = index < first + width
+        rest = jnp.where((lane >= first) & (lane < first + width), 0.0, rest)
         for k in range(width):
             here = lane == first + k
-            pivot = cols[k][k : k + 1, :]
-            factor = jnp.where(index > k, cols[k] * (1.0 / pivot), 0.0)
+            pivot = heads[k][k : k + 1, :]
+            inverse = 1.0 / pivot
+            factor = jnp.where(done, 0.0, cols[k] * inverse)
+            head = jnp.where(inner > k, heads[k] * inverse, 0.0)
             unit = jnp.where(here, 1.0, panel[k : k + 1, :])
-            linv[first + k : first + k + 1, :] = (
+            linv[pl.ds(first + k, 1), :] = (
                 jnp.where(lane <= first + k, unit, 0.0) * lax.rsqrt(pivot)
             )
             if k + 1 < width:
-                panel = jnp.where(here, 0.0, panel) - factor[0:8, :] * unit
+                panel = jnp.where(here, 0.0, panel) - head * unit
             for later in range(k + 1, width):
-                cols[later] = cols[later] - factor * cols[k][later : later + 1, :]
+                other = heads[k][later : later + 1, :]
+                cols[later] = cols[later] - factor * other
+                heads[later] = heads[later] - head * other
             inside = (lane > first + k) & (lane < first + width)
             rest = rest - factor * jnp.where(inside, 0.0, unit)
-        if n > width:
-            work[pl.ds(first + width, n - width), :] = rest[width:, :]
-
-    for first in range(0, rank // 2, width):
-        eliminate(first, width)
+        work[top:, :] = rest
+
+    def eliminate_from(top, end):
+        loop(top // width, end // width, lambda i: eliminate(top, i * width))
+
+    eliminate_from(0, rank // 2)
 
     arrive(ub)
     u2s[...] = ut[b] + ulb[0] + ulb[1]
-    for first in range(rank // 2, rank, width):
-        eliminate(first, width)
+    eliminate_from(rank // 2, rank)
 
     li = linv[...]
     for k in (*range(na // 2, na), *range(1, na // 2), 0):

time: 136 us -> 137 us (level)
    pallas_call x1, Pallas kernels: 130 us -> 131 us  [per_device(): pl.pallas_call(functools.partial(kernel, n_section, nz, rank), out_shape=...]
where the time goes in v2:
time: 137 us; the launch traced here: 135 us
  Pallas kernels  131 us (96%)
  local copies, waits for them, and re-layouts  2.29 us (2%)
  other arithmetic  1.41 us (1%)
    pallas_call x1, Pallas kernels, per_device(): pl.pallas_call(functools.partial(kernel, n_section, nz, rank), out_shape=...  131 us

profile of v2, /device:TPU:6, one launch (start us, length us, event | category | flops | bytes accessed | tf_op | source)
XLA Modules:
  0.0 135.4 jit_solution(13231319887026857863)
XLA Ops:
  0.6 131.1 %shard_map.112 = (bf16[128,4096]{1,0:T(8,128)(2,1)}, bf16[128,128]{1,0:T(8,128)(2,1)}, bf16[128,128]{1,0:T(8,128)(2,1)}) custom-call(s32[1,2]{1,0:T(1,128)} %lens.1, f32[1,4096]{1,0:T(1,128)} %gain_in.1, bf16[128,4096]{1,0:T(8,128)(2,1)} %bitcast.12, bf16[128,4096]{1,0:T(8,128)(2,1)} %bitcast.13, bf16[128,512]{1,0:T(8,128)(2,1)} %bitcast.15, ...), custom_call_target="tpu_custom_call" | custom-call | tf_op jit(solution)/shard_map/pallas_call | solution.py:577
  131.7 1.4 %select_bitcast_fusion = (bf16[1,128,128]{2,1,0:T(8,128)(2,1)}, bf16[1,128,128]{2,1,0:T(8,128)(2,1)}) fusion(bf16[128,128]{1,0:T(8,128)(2,1)} %get-tuple-element.8, pred[]{:T(512)S(6)} %lt.3, bf16[128,128]{1,0:T(8,128)(2,1)} %get-tuple-element.7), kind=kLoop, calls=%fused_computation | loop fusion | flops 32768 | bytes 131073 | tf_op jit(solution)/shard_map/broadcast_in_dim | solution.py:600
  133.1 2.3 %copy.13 = bf16[1,128,4096]{2,1,0:T(8,128)(2,1)} copy(bf16[1,128,4096]{2,1,0:T(8,128)(2,1)} %bitcast.14) | data formatting | bytes 2097152

commit v3 on v1

--- a/solution.py
+++ b/solution.py
@@ -33,9 +33,9 @@
     n_section, nz, rank, lens, gain_in, saved, err, down, up, left, right, warm,
     out_ne, out_l, out_r,
     gain, xall, xoth, eall, lall, upv, dall, rw, ivb,
-    mpart, ml1, m2s, ml2, mxs, mxr, mown, mfull,
+    mpart, mhalf, ml1, m2s, ml2, mxs, mxr, mown, mfull,
     xg, prs, prr, pre_ref, dpre_ref, mom, mom16, pjs, pjr, pj,
-    gpart, gl1, g2s, gl2, gfull, work, linv, ut, ula, ulb, u2s, un, ul2, rt, ph16, rown, neb,
+    gpart, gl1, g2s, gl2, gfull, work, linv, ut, ula, ulb, u2s, ul2, rt, ph16, rown, neb,
     ld_sem, x_send, x_recv, a_send, a_recv,
     m_send, m_recv, g_send, g_recv, u_send, u_recv, r_send, r_recv, q_send, q_recv,
     ne_send, ne_recv, ne_loc, sec_send, sec_recv,
@@ -160,16 +160,20 @@
     loads[3].wait()
     x_left = across(1, lall.at[mine], lall.at[mine])
     x_left.start()
+    loads[5].wait()
+
+    mh, mb, ms = rl // 2, rl // 2 // nb, rl // 2 // nz
+    mpart[...] = nn(upv[...], rw[z, 0])
+    mxs[...] = mpart[rows(o * mh, mh), :].astype(BF16)
+    x_m = across(4, mxs, mxr)
+    x_m.start()
     loads[4].wait()
     x_saved = across(0, xoth, xall.at[mine])
     x_saved.start()
-    loads[5].wait()
-
-    mb, ms = rl // nb, rl // nz
-    mpart[...] = nn(upv[...], rw[z, 0]).astype(BF16)
-    my_m = rows(b * mb + a * ms, ms)
-    my_mb = rows(b * mb, mb)
-    m1 = [near(k, mpart.at[rows(near_b(k) * mb, mb)], ml1.at[k], m_send.at[0, k], m_recv.at[0, k])
+    my_mh = rows(x * mh, mh)
+    my_mb = pl.ds(pl.multiple_of(x * mh + b * mb, mb), mb)
+    my_m = pl.ds(pl.multiple_of(x * mh + b * mb + a * ms, ms), ms)
+    m1 = [near(k, mhalf.at[rows(near_b(k) * mb, mb)], ml1.at[k], m_send.at[0, k], m_recv.at[0, k])
           for k in range(1, nb)]
     m2 = [far(k, m2s.at[rows(far_a(k) * ms, ms)], ml2.at[k], m_send.at[1, k], m_recv.at[1, k])
           for k in range(1, na)]
@@ -185,7 +189,6 @@
         for copy in copies:
             copy.wait_recv()
 
-    start(m1)
     x_err = across(2, err.at[:, other_half], eall.at[mine])
     x_err.start()
 
@@ -225,33 +228,36 @@
         if t >= lag:
             advance(1, t - lag)
         if t == steps // 8:
+            x_m.wait_recv()
+            mhalf[...] = (mpart[my_mh, :] + mxr[...].astype(F32)).astype(BF16)
+            start(m1)
+        if t == 3 * steps // 8:
             arrive(m1)
-            msum = mpart[my_mb, :].astype(F32)
+            msum = mhalf[rows(b * mb, mb), :].astype(F32)
             for k in range(1, nb):
                 msum = msum + ml1[k].astype(F32)
             m2s[...] = msum.astype(BF16)
             start(m2)
-        if t == 3 * steps // 8:
+        if t == 5 * steps // 8:
             arrive(m2)
             msum = m2s[rows(a * ms, ms), :].astype(F32)
             for k in range(1, na):
                 msum = msum + ml2[k].astype(F32)
-            mxs[...] = msum
-            x_m = across(4, mxs, mxr)
-            x_m.start()
+            mown[...] = msum.astype(BF16)
+            mfull[my_m, :] = mown[...]
+            start(m3)
         if t == steps // 2:
             x_saved.wait_recv()
             loads[8].wait()
             loop(0, n_chunk, scale)
             pre_ref[...] = term(z)
-        if t == 5 * steps // 8:
-            x_m.wait_recv()
-            mown[...] = (mxs[...] + mxr[...]).astype(BF16)
-            mfull[my_m, :] = mown[...]
-            start(m3)
         if t == 6 * steps // 8:
             arrive(m3)
             start(m4)
+        if t == 7 * steps // 8:
+            arrive(m4)
+            x_m2 = across(7, mfull.at[my_mh], mfull.at[my_mh])
+            x_m2.start()
         if t >= steps // 2:
             first = 2 * (t - steps // 2)
             found = [term(block) for step in (first, first + 1) for block in blocks_of(step)]
@@ -269,7 +275,7 @@
             for block in blocks_of(step):
                 mom[:, rows(block * tok, tok)] = nt(lall[...], rw[block, 0])
     x_inv.wait_recv()
-    arrive(m4)
+    x_m2.wait_recv()
     dact = nt(lall[...], mfull[...])
     inv = ivb[:, 0:1]
     slot = z * tok + lax.broadcasted_iota(jnp.int32, (2 * tok, 1), 0)
@@ -338,7 +344,7 @@
         send_to(to_right, ut.at[near_b(1)], ulb.at[0], u_send.at[2], u_recv.at[2]),
         send_to(to_left, ut.at[near_b(3)], ulb.at[1], u_send.at[3], u_recv.at[3]),
     ]
-    u2 = [far(k, un.at[far_a(k)], ul2.at[k], u_send.at[3 + k], u_recv.at[3 + k])
+    u2 = [far(k, u2s.at[far_a(k)], ul2.at[k], u_send.at[3 + k], u_recv.at[3 + k])
           for k in range(1, na)]
 
     moment_terms(2)
@@ -351,17 +357,20 @@
     start(g2)
     moment_terms(1)
     moment_terms(3)
+    arrive(ua)
+    ut[near_b(1), first_half] += ula[0]
+    ut[near_b(3), last_half] += ula[1]
+    start(ub)
+    moment_terms(0)
     arrive(g2)
     gsum = g2s[...]
     for k in range(1, na):
         gsum = gsum + gl2[k]
     gfull[my_gb, :] = gsum
     start(g3)
-    arrive(ua)
-    ut[near_b(1), first_half] += ula[0]
-    ut[near_b(3), last_half] += ula[1]
-    start(ub)
-    moment_terms(0)
+    arrive(ub)
+    u2s[...] = ut[b] + ulb[0] + ulb[1]
+    start(u2)
     arrive(g3)
     work[...] = gfull[...]
 
@@ -394,19 +403,18 @@
         if n > width:
             work[pl.ds(first + width, n - width), :] = rest[width:, :]
 
-    for first in range(0, rank // 2, width):
+    for first in range(0, rank, width):
         eliminate(first, width)
 
-    arrive(ub)
-    u2s[...] = ut[b] + ulb[0] + ulb[1]
-    for first in range(rank // 2, rank, width):
-        eliminate(first, width)
-
     li = linv[...]
-    for k in (*range(na // 2, na), *range(1, na // 2), 0):
-        un[far_a(k)] = nn(li, u2s[far_a(k)], HIGHEST).astype(BF16)
-        if k > 0:
-            u2[k - 1].start()
+    arrive(u2)
+    usum = u2s[a]
+    for k in range(1, na):
+        usum = usum + ul2[k]
+    right_t = nn(li, usum, HIGHEST)
+    rt[b, a] = right_t.astype(BF16)
+    r1 = [far(k, rt.at[b, a], rt.at[b, a], r_send.at[k], r_recv.at[k]) for k in range(1, na)]
+    start(r1)
     ph16[...] = nt(pj[...], li, HIGHEST).astype(BF16)
     to_prev = {"section": s_prev}
     outs = [
@@ -414,14 +422,6 @@
         send_to(to_prev, rown, out_r, sec_send.at[1], sec_recv.at[1]),
     ]
     outs[0].start()
-    arrive(u2)
-    right_t = un[a].astype(F32)
-    for k in range(1, na):
-        right_t = right_t + ul2[k].astype(F32)
-    rt[b, a] = right_t.astype(BF16)
-
-    r1 = [far(k, rt.at[b, a], rt.at[b, a], r_send.at[k], r_recv.at[k]) for k in range(1, na)]
-
     def pass_on(device, view, i):
         return send_to(device, rt.at[view], rt.at[view], q_send.at[i], q_recv.at[i])
 
@@ -429,7 +429,6 @@
     rb_left = [pass_on(to_left, (b, first_half), 2), pass_on(to_left, (b, last_half), 3)]
     rc_right = pass_on(to_right, (near_b(3), first_half), 4)
     rc_left = pass_on(to_left, (near_b(1), last_half), 5)
-    start(r1)
     rown[...] = right_t.T.astype(BF16)
     outs[1].start()
     arrive(r1)
@@ -470,7 +469,7 @@
     own = pltpu.make_async_copy(neb.at[mine], out_ne.at[:, my_half], ne_loc)
     own.start()
 
-    for copy in (x_saved, x_left, x_err, x_inv, x_m, x_pre, x_pj):
+    for copy in (x_saved, x_left, x_err, x_inv, x_m, x_m2, x_pre, x_pj):
         copy.wait_send()
     for copies in (
         m1, m2, m3, m4, g1, g2, g3, ua, ub, u2, r1, rb_right, rb_left, [rc_right, rc_left],
@@ -517,13 +516,14 @@
         vmem((half, rl), BF16),
         vmem((nz, 2, tok, rank), BF16),
         vmem((2 * tok, 128), F32),
-        vmem((rl, rank), BF16),
-        vmem((nb, rl // nb, rank), BF16),
-        vmem((rl // nb, rank), BF16),
-        vmem((na, rl // nz, rank), BF16),
-        vmem((rl // nz, rank), F32),
-        vmem((rl // nz, rank), F32),
-        vmem((rl // nz, rank), BF16),
+        vmem((rl, rank), F32),
+        vmem((rl // 2, rank), BF16),
+        vmem((nb, rl // 2 // nb, rank), BF16),
+        vmem((rl // 2 // nb, rank), BF16),
+        vmem((na, rl // 2 // nz, rank), BF16),
+        vmem((rl // 2, rank), BF16),
+        vmem((rl // 2, rank), BF16),
+        vmem((rl // 2 // nz, rank), BF16),
         vmem((rl, rank), BF16),
         vmem((2 * tok, half), BF16),
         vmem((2 * tok, rl), BF16),
@@ -546,13 +546,12 @@
         vmem((2, na // 2, rank, tok), F32),
         vmem((2, na, rank, tok), F32),
         vmem((na, rank, tok), F32),
-        vmem((na, rank, tok), BF16),
-        vmem((na, rank, tok), BF16),
+        vmem((na, rank, tok), F32),
         vmem((nb, na, rank, tok), BF16),
         vmem((2 * tok, rank), BF16),
         vmem((tok, rank), BF16),
         vmem((2 * tok, half), BF16),
-        dma((9,)), dma((7,)), dma((7,)),
+        dma((9,)), dma((8,)), dma((8,)),
         dma((2, 2, steps)), dma((2, 2, steps)),
         dma((4, 4)), dma((4, 4)), dma((4, 4)), dma((4, 4)),
         dma((8,)), dma((8,)), dma((4,)), dma((4,)), dma((6,)), dma((6,)),

time: 136 us -> 134 us (0.985); the launches traced: 134 us -> 133 us
  no operation moved by 1% of the time
where the time goes in v3:
time: 134 us; the launch traced here: 133 us
  Pallas kernels  129 us (96%)
  local copies, waits for them, and re-layouts  2.29 us (2%)
  other arithmetic  1.41 us (1%)
    pallas_call x1, Pallas kernels, per_device(): pl.pallas_call(functools.partial(kernel, n_section, nz, rank), out_shape=...  129 us

profile of v3, /device:TPU:6, one launch (start us, length us, event | category | flops | bytes accessed | tf_op | source)
XLA Modules:
  0.0 133.4 jit_solution(14382573773805690183)
XLA Ops:
  0.6 129.0 %shard_map.112 = (bf16[128,4096]{1,0:T(8,128)(2,1)}, bf16[128,128]{1,0:T(8,128)(2,1)}, bf16[128,128]{1,0:T(8,128)(2,1)}) custom-call(s32[1,2]{1,0:T(1,128)} %lens.1, f32[1,4096]{1,0:T(1,128)} %gain_in.1, bf16[128,4096]{1,0:T(8,128)(2,1)} %bitcast.12, bf16[128,4096]{1,0:T(8,128)(2,1)} %bitcast.13, bf16[128,512]{1,0:T(8,128)(2,1)} %bitcast.15, ...), custom_call_target="tpu_custom_call" | custom-call | tf_op jit(solution)/shard_map/pallas_call | solution.py:560
  129.7 1.4 %select_bitcast_fusion = (bf16[1,128,128]{2,1,0:T(8,128)(2,1)}, bf16[1,128,128]{2,1,0:T(8,128)(2,1)}) fusion(bf16[128,128]{1,0:T(8,128)(2,1)} %get-tuple-element.8, pred[]{:T(512)S(6)} %lt.3, bf16[128,128]{1,0:T(8,128)(2,1)} %get-tuple-element.7), kind=kLoop, calls=%fused_computation | loop fusion | flops 32768 | bytes 131073 | tf_op jit(solution)/shard_map/broadcast_in_dim | solution.py:583
  131.1 2.3 %copy.13 = bf16[1,128,4096]{2,1,0:T(8,128)(2,1)} copy(bf16[1,128,4096]{2,1,0:T(8,128)(2,1)} %bitcast.14) | data formatting | bytes 2097152

commit v4 on v3

--- a/solution.py
+++ b/solution.py
@@ -32,10 +32,10 @@
 def kernel(
     n_section, nz, rank, lens, gain_in, saved, err, down, up, left, right, warm,
     out_ne, out_l, out_r,
-    gain, xall, xoth, eall, lall, upv, dall, rw, ivb,
+    gain, xall, xoth, eall, lall, upv, dall, rw, ivb, ivs, ivr,
     mpart, mhalf, ml1, m2s, ml2, mxs, mxr, mown, mfull,
     xg, prs, prr, pre_ref, dpre_ref, mom, mom16, pjs, pjr, pj,
-    gpart, gl1, g2s, gl2, gfull, work, linv, ut, ula, ulb, u2s, ul2, rt, ph16, rown, neb,
+    gpart, gl1, g2s, gl2, gfull, work, linv, beyond, ut, ula, ulb, u2s, ul2, rt, ph16, rown, neb,
     ld_sem, x_send, x_recv, a_send, a_recv,
     m_send, m_recv, g_send, g_recv, u_send, u_recv, r_send, r_recv, q_send, q_recv,
     ne_send, ne_recv, ne_loc, sec_send, sec_recv,
@@ -199,8 +199,10 @@
         for v in (xoth[:, cols], xall[mine, cols]):
             v = v.astype(F32)
             total = total + jnp.sum(v * v, axis=1, keepdims=True)
-    ivb[mine, :] = jnp.broadcast_to(lax.rsqrt(total * (1.0 / feat) + 1e-05), (tok, 128))
-    x_inv = across(3, ivb.at[mine], ivb.at[mine])
+    inv_own = jnp.broadcast_to(lax.rsqrt(total * (1.0 / feat) + 1e-05), (tok, 128))
+    ivb[mine, :] = inv_own
+    ivs[...] = inv_own.T[0:8, :]
+    x_inv = across(3, ivs, ivr)
     x_inv.start()
 
     gain_off = x * half
@@ -275,6 +277,7 @@
             for block in blocks_of(step):
                 mom[:, rows(block * tok, tok)] = nt(lall[...], rw[block, 0])
     x_inv.wait_recv()
+    ivb[theirs, :] = jnp.broadcast_to(ivr[0:1, :], (tok, 128)).T
     x_m2.wait_recv()
     dact = nt(lall[...], mfull[...])
     inv = ivb[:, 0:1]
@@ -375,27 +378,29 @@
     work[...] = gfull[...]
 
     lane = lax.broadcasted_iota(jnp.int32, (1, rank), 1)
-    group, width = 16, 8
-
-    def eliminate(first, width):
-        n = rank - first
+    block, width = 32, 16
+
+    def eliminate(first, width, end):
+        n = end - first
         a = work[pl.ds(first, n), :]
         index = lax.broadcasted_iota(jnp.int32, (n, rank), 0)
         cols = [
             jnp.broadcast_to(a[:, first + k : first + k + 1], (n, rank)) for k in range(width)
         ]
-        panel = a[0:8, :]
+        panel = a[0:width, :]
         rest = jnp.where((lane >= first) & (lane < first + width), 0.0, a)
         for k in range(width):
             here = lane == first + k
             pivot = cols[k][k : k + 1, :]
             factor = jnp.where(index > k, cols[k] * (1.0 / pivot), 0.0)
             unit = jnp.where(here, 1.0, panel[k : k + 1, :])
-            linv[first + k : first + k + 1, :] = (
-                jnp.where(lane <= first + k, unit, 0.0) * lax.rsqrt(pivot)
+            scaled = unit * lax.rsqrt(pivot)
+            linv[first + k : first + k + 1, :] = jnp.where(lane <= first + k, scaled, 0.0)
+            beyond[first + k - (end - block) : first + k + 1 - (end - block), :] = (
+                jnp.where(lane >= end, scaled, 0.0)
             )
             if k + 1 < width:
-                panel = jnp.where(here, 0.0, panel) - factor[0:8, :] * unit
+                panel = jnp.where(here, 0.0, panel) - factor[0:width, :] * unit
             for later in range(k + 1, width):
                 cols[later] = cols[later] - factor * cols[k][later : later + 1, :]
             inside = (lane > first + k) & (lane < first + width)
@@ -403,8 +408,14 @@
         if n > width:
             work[pl.ds(first + width, n - width), :] = rest[width:, :]
 
-    for first in range(0, rank, width):
-        eliminate(first, width)
+    for end in range(block, rank + 1, block):
+        for first in range(end - block, end, width):
+            eliminate(first, width, end)
+        if end < rank:
+            over = beyond[...]
+            update = nn(over.T, over + linv[end - block : end, :], HIGHEST)
+            mine_below = jnp.where((lane >= end - block) & (lane < end), 0.0, work[end:, :])
+            work[end:, :] = mine_below - update[end:, :]
 
     li = linv[...]
     arrive(u2)
@@ -516,6 +527,8 @@
         vmem((half, rl), BF16),
         vmem((nz, 2, tok, rank), BF16),
         vmem((2 * tok, 128), F32),
+        vmem((8, tok), F32),
+        vmem((8, tok), F32),
         vmem((rl, rank), F32),
         vmem((rl // 2, rank), BF16),
         vmem((nb, rl // 2 // nb, rank), BF16),
@@ -542,6 +555,7 @@
         vmem((rank, rank), F32),
         vmem((rank, rank), F32),
         vmem((rank, rank), F32),
+        vmem((32, rank), F32),
         vmem((nb, na, rank, tok), F32),
         vmem((2, na // 2, rank, tok), F32),
         vmem((2, na, rank, tok), F32),

time: 134 us -> 134 us (level)
  no operation moved by 1% of the time
where the time goes in v4:
time: 134 us
  Pallas kernels  129 us (96%)
  local copies, waits for them, and re-layouts  2.29 us (2%)
  other arithmetic  1.41 us (1%)
    pallas_call x1, Pallas kernels, per_device(): pl.pallas_call(functools.partial(kernel, n_section, nz, rank), out_shape=...  129 us

profile of v4, /device:TPU:6, one launch (start us, length us, event | category | flops | bytes accessed | tf_op | source)
XLA Modules:
  0.0 133.6 jit_solution(1986854483047322475)
XLA Ops:
  0.6 129.3 %shard_map.112 = (bf16[128,4096]{1,0:T(8,128)(2,1)}, bf16[128,128]{1,0:T(8,128)(2,1)}, bf16[128,128]{1,0:T(8,128)(2,1)}) custom-call(s32[1,2]{1,0:T(1,128)} %lens.1, f32[1,4096]{1,0:T(1,128)} %gain_in.1, bf16[128,4096]{1,0:T(8,128)(2,1)} %bitcast.12, bf16[128,4096]{1,0:T(8,128)(2,1)} %bitcast.13, bf16[128,512]{1,0:T(8,128)(2,1)} %bitcast.15, ...), custom_call_target="tpu_custom_call" | custom-call | tf_op jit(solution)/shard_map/pallas_call | solution.py:574
  129.9 1.4 %select_bitcast_fusion = (bf16[1,128,128]{2,1,0:T(8,128)(2,1)}, bf16[1,128,128]{2,1,0:T(8,128)(2,1)}) fusion(bf16[128,128]{1,0:T(8,128)(2,1)} %get-tuple-element.8, pred[]{:T(512)S(6)} %lt.3, bf16[128,128]{1,0:T(8,128)(2,1)} %get-tuple-element.7), kind=kLoop, calls=%fused_computation | loop fusion | flops 32768 | bytes 131073 | tf_op jit(solution)/shard_map/broadcast_in_dim | solution.py:597
  131.4 2.3 %copy.13 = bf16[1,128,4096]{2,1,0:T(8,128)(2,1)} copy(bf16[1,128,4096]{2,1,0:T(8,128)(2,1)} %bitcast.14) | data formatting | bytes 2097152

commit v5 on v4

--- a/solution.py
+++ b/solution.py
@@ -35,7 +35,7 @@
     gain, xall, xoth, eall, lall, upv, dall, rw, ivb, ivs, ivr,
     mpart, mhalf, ml1, m2s, ml2, mxs, mxr, mown, mfull,
     xg, prs, prr, pre_ref, dpre_ref, mom, mom16, pjs, pjr, pj,
-    gpart, gl1, g2s, gl2, gfull, work, linv, beyond, ut, ula, ulb, u2s, ul2, rt, ph16, rown, neb,
+    gpart, gl1, g2s, gl2, gfull, work, linv, beyond, ut, ula, ulb, u2s, ulc, ul2, rt, ph16, rown, neb,
     ld_sem, x_send, x_recv, a_send, a_recv,
     m_send, m_recv, g_send, g_recv, u_send, u_recv, r_send, r_recv, q_send, q_recv,
     ne_send, ne_recv, ne_loc, sec_send, sec_recv,
@@ -347,8 +347,15 @@
         send_to(to_right, ut.at[near_b(1)], ulb.at[0], u_send.at[2], u_recv.at[2]),
         send_to(to_left, ut.at[near_b(3)], ulb.at[1], u_send.at[3], u_recv.at[3]),
     ]
-    u2 = [far(k, u2s.at[far_a(k)], ul2.at[k], u_send.at[3 + k], u_recv.at[3 + k])
-          for k in range(1, na)]
+    between = na == 4
+    top, bottom = pl.ds(0, rank // 2), pl.ds(rank // 2, rank // 2)
+    uc = [
+        far(k, u2s.at[far_a(2), part], ulc.at[i], u_send.at[6 + i], u_recv.at[6 + i])
+        for i, (k, part) in enumerate([(1, top), (3, bottom)])
+    ] if between else []
+    last_k = (1, 3) if between else tuple(range(1, na))
+    u2 = [far(k, u2s.at[far_a(k)], ul2.at[k], u_send.at[3 + k - k // 3], u_recv.at[3 + k - k // 3])
+          for k in last_k]
 
     moment_terms(2)
     start(ua)
@@ -373,7 +380,7 @@
     start(g3)
     arrive(ub)
     u2s[...] = ut[b] + ulb[0] + ulb[1]
-    start(u2)
+    start(uc if between else u2)
     arrive(g3)
     work[...] = gfull[...]
 
@@ -416,11 +423,16 @@
             update = nn(over.T, over + linv[end - block : end, :], HIGHEST)
             mine_below = jnp.where((lane >= end - block) & (lane < end), 0.0, work[end:, :])
             work[end:, :] = mine_below - update[end:, :]
+        if between and end == rank // 2:
+            arrive(uc)
+            u2s[far_a(1), top] += ulc[0]
+            u2s[far_a(3), bottom] += ulc[1]
+            start(u2)
 
     li = linv[...]
     arrive(u2)
     usum = u2s[a]
-    for k in range(1, na):
+    for k in last_k:
         usum = usum + ul2[k]
     right_t = nn(li, usum, HIGHEST)
     rt[b, a] = right_t.astype(BF16)
@@ -483,7 +495,7 @@
     for copy in (x_saved, x_left, x_err, x_inv, x_m, x_m2, x_pre, x_pj):
         copy.wait_send()
     for copies in (
-        m1, m2, m3, m4, g1, g2, g3, ua, ub, u2, r1, rb_right, rb_left, [rc_right, rc_left],
+        m1, m2, m3, m4, g1, g2, g3, ua, ub, uc, u2, r1, rb_right, rb_left, [rc_right, rc_left],
     ):
         for copy in copies:
             copy.wait_send()
@@ -560,6 +572,7 @@
         vmem((2, na // 2, rank, tok), F32),
         vmem((2, na, rank, tok), F32),
         vmem((na, rank, tok), F32),
+        vmem((2, rank // 2, tok), F32),
         vmem((na, rank, tok), F32),
         vmem((nb, na, rank, tok), BF16),
         vmem((2 * tok, rank), BF16),

time: 134 us -> 133 us (level)
  Pallas kernels: 129 us -> 127 us
    pallas_call x1, Pallas kernels: 129 us -> 127 us  [per_device(): pl.pallas_call(functools.partial(kernel, n_section, nz, rank), out_shape=...]
where the time goes in v5:
time: 133 us; the launch traced here: 132 us
  Pallas kernels  127 us (95%)
  local copies, waits for them, and re-layouts  2.29 us (2%)
  other arithmetic  1.41 us (1%)
    pallas_call x1, Pallas kernels, per_device(): pl.pallas_call(functools.partial(kernel, n_section, nz, rank), out_shape=...  127 us

profile of v5, /device:TPU:6, one launch (start us, length us, event | category | flops | bytes accessed | tf_op | source)
XLA Modules:
  0.0 131.8 jit_solution(8582797574543962581)
XLA Ops:
  0.6 127.5 %shard_map.112 = (bf16[128,4096]{1,0:T(8,128)(2,1)}, bf16[128,128]{1,0:T(8,128)(2,1)}, bf16[128,128]{1,0:T(8,128)(2,1)}) custom-call(s32[1,2]{1,0:T(1,128)} %lens.1, f32[1,4096]{1,0:T(1,128)} %gain_in.1, bf16[128,4096]{1,0:T(8,128)(2,1)} %bitcast.12, bf16[128,4096]{1,0:T(8,128)(2,1)} %bitcast.13, bf16[128,512]{1,0:T(8,128)(2,1)} %bitcast.15, ...), custom_call_target="tpu_custom_call" | custom-call | tf_op jit(solution)/shard_map/pallas_call | solution.py:587
  128.1 1.4 %select_bitcast_fusion = (bf16[1,128,128]{2,1,0:T(8,128)(2,1)}, bf16[1,128,128]{2,1,0:T(8,128)(2,1)}) fusion(bf16[128,128]{1,0:T(8,128)(2,1)} %get-tuple-element.8, pred[]{:T(512)S(6)} %lt.3, bf16[128,128]{1,0:T(8,128)(2,1)} %get-tuple-element.7), kind=kLoop, calls=%fused_computation | loop fusion | flops 32768 | bytes 131073 | tf_op jit(solution)/shard_map/broadcast_in_dim | solution.py:610
  129.5 2.3 %copy.13 = bf16[1,128,4096]{2,1,0:T(8,128)(2,1)} copy(bf16[1,128,4096]{2,1,0:T(8,128)(2,1)} %bitcast.14) | data formatting | bytes 2097152
